TPU v7x, 128 devices: a whole 4x4x4 slice. The times are simulated.
128 devices in a mesh: lon: 32 (over y, x_hi, z), lat: 4 (over x_lo, core).
Axes of the slice: x: 4 (x_hi: 2, x_lo: 2; x = x_hi * 2 + x_lo), y: 4, z: 4, core: 2. Of those that a mesh axis runs over, the one named last changes fastest.
Arguments:
- tracers: float32 [2, 10, 256, 16384], P(None, None, 'lat', 'lon'), may hold values from -6 to 6
- diffusivity: float32 [3, 10, 256, 16384], P(None, None, 'lat', 'lon'), may hold values from 0.02 to 0.12
- velocity: float32 [2, 10, 256, 16384], P(None, None, 'lat', 'lon'), may hold values from -0.16 to 0.16
- wet_mask: int32 [10, 256, 16384], P(None, 'lat', 'lon'), may hold values 0 or 1
- argo_rows: float32 [16384, 128], P(('lon', 'lat')), may hold values from -6 to 6
- argo_dest: int32 [16384, 1], P(('lon', 'lat')), may hold values from 0 to 127; in each aligned block of 128 rows (0 to 127, 128 to 255, ...) at most 2 rows name the same one
- argo_cols: int32 [16384], P(('lon', 'lat')), may hold values from 0 to 32767
- argo_count: int32 [128], P(('lon', 'lat')), may hold values from 96 to 128
- float_values: float32 [2048, 2, 128], P(('lon', 'lat')), may hold values from -6 to 6
- float_pos: float32 [2048, 2, 128], P(('lon', 'lat')), may hold values from 0 to 0.999
- float_dest: int32 [2048, 1], P(('lon', 'lat')), may hold values from 0 to 4; in each aligned block of 16 rows (0 to 15, 16 to 31, ...) at most 4 rows name the same one
Outputs:
- fields: float32 [2, 10, 256, 16384], P(None, None, 'lat', 'lon')
- floats_out: float32 [2560, 2, 128], P(('lon', 'lat'))
Inputs may be any that keep to these rules, and one draw needn't show every extreme that they name: `argo_dest`: in the rows of one tile no tile is named more than 2 times, a bound that some block reaches. `float_dest`: in the rows of one tile no direction is named more than 4 times, a bound that some block reaches.
All inputs are finite; a program needn't handle non-finite values. No bound on the sum of `wet_mask` on one device may be relied on, other than what follows from the above.
Results may differ from a plain program's by a relative error of at most 0.0003.
Values sent between devices are 32-bit elements; how exact they have to be, the bound alone decides.
A program may use at most 128 MiB of HBM per device.

v0:
```python
import functools

import jax
import jax.numpy as jnp
from jax import lax
from jax.experimental import pallas as pl
from jax.experimental.pallas import tpu as pltpu
from jax.sharding import PartitionSpec as P

MESH = pl.DeviceIdType.MESH
F32, BF16, I32 = jnp.float32, jnp.bfloat16, jnp.int32

LEVELS, H, W = 10, 64, 512
EH, EW = 72, 640
STRIPS = EH // 8
PAY = 21


def split(x):
    high = x.astype(BF16)
    return high, (x - high.astype(F32)).astype(BF16)


def iota(shape, dim):
    return lax.broadcasted_iota(I32, shape, dim)


def column_of(row):
    n = row.shape[1]
    wide = jnp.broadcast_to(row, (n, n))
    return jnp.sum(jnp.where(iota((n, n), 0) == iota((n, n), 1), wide, 0.0), axis=1, keepdims=True)


def ranks_of(row):
    n = row.shape[1]
    earlier = (column_of(row) == row) & (iota((n, n), 0) < iota((n, n), 1))
    return jnp.sum(earlier.astype(F32), axis=0, keepdims=True)


def places():
    lon, lat = lax.axis_index("lon"), lax.axis_index("lat")
    z, b = lon % 4, lon // 4
    u, v = (b % 2) * 4 + lat, (b // 2) * 4 + z
    return lon, lat, u, v


def device_of(u, v):
    return ((v // 4) * 8 + (u // 4) * 4 + v % 4, u % 4)


def kernel(
    tr_hbm, di_hbm, ve_hbm, wet_hbm, rows_ref, dest_ref, cols_ref, count_ref, fval_ref, fpos_ref, fdest_ref,
    out_ref, fout_ref,
    c0, c1, dx, vx, wi, wf, vbuf, packs, from_w, from_e, from_nw, from_sw, from_ne, from_se,
    msg, mid, got, fsend, fgot, amat, hot,
    load_sem, p1_s, p1_r, p2_s, p2_r, ns_s, ns_r, ew_s, ew_r, fl_s, fl_r,
):
    lon, lat, u, v = places()
    east, west = ((lon + 1) % 32, lat), ((lon + 31) % 32, lat)
    north, south = (lon, (lat + 1) % 4), (lon, (lat + 3) % 4)
    ne, se = (east[0], north[1]), (east[0], south[1])
    nw, sw = (west[0], north[1]), (west[0], south[1])
    barrier = pltpu.get_barrier_semaphore()

    @pl.loop(1, 8)
    def _(d):
        pl.semaphore_signal(barrier, inc=1, device_id=device_of((u + d) % 8, v), device_id_type=MESH)

    @pl.loop(1, 16)
    def _(d):
        pl.semaphore_signal(barrier, inc=1, device_id=device_of(u, (v + d) % 16), device_id_type=MESH)

    for peer in (east, west, north, south, ne, se, nw, sw):
        pl.semaphore_signal(barrier, inc=1, device_id=peer, device_id_type=MESH)

    loads = [
        pltpu.make_async_copy(di_hbm, dx.at[:, :, pl.ds(0, H), pl.ds(0, W)], load_sem.at[0]),
        pltpu.make_async_copy(ve_hbm, vx.at[:, :, pl.ds(0, H), pl.ds(0, W)], load_sem.at[1]),
        pltpu.make_async_copy(wet_hbm, wi.at[:, pl.ds(0, H)], load_sem.at[2]),
        pltpu.make_async_copy(tr_hbm, c0.at[:, pl.ds(0, LEVELS), pl.ds(0, H), pl.ds(0, W)], load_sem.at[3]),
    ]
    for copy in loads:
        copy.start()

    lane = iota((128, 128), 1)
    sub = iota((128, 128), 0)
    level = jnp.where(sub >= PAY, sub - PAY, sub)
    tracer = jnp.where(level >= LEVELS, 1, 0)
    level = level - tracer * LEVELS
    depth = lane - tracer * 64
    weight = jnp.maximum(0.0, 1.0 - jnp.abs(depth.astype(F32) * ((LEVELS - 1) / 63.0) - level.astype(F32)))
    weight = jnp.where((depth >= 0) & (depth < 64), weight, 0.0)
    total = jnp.sum(weight, axis=1, keepdims=True)
    table = 0.5 * weight / jnp.where(total > 0.0, total, 1.0)
    pay = lax.dot_general(
        table, rows_ref[...], (((1,), (1,)), ((), ())), precision=lax.Precision.HIGHEST, preferred_element_type=F32
    )
    cell = (cols_ref[...] + 1).astype(F32)
    pay = jnp.where((sub == PAY - 1) | (sub == 2 * PAY - 1), jnp.broadcast_to(cell, (128, 128)), pay)
    pay = jnp.concatenate([jnp.where(sub < PAY, pay, 0.0), jnp.where((sub >= PAY) & (sub < 2 * PAY), pay, 0.0)], axis=1)
    live = iota((1, 128), 1) < count_ref[0]
    dest = jnp.where(live, dest_ref[...], -5).astype(F32)
    rank = ranks_of(dest)
    tile = ((sub % 32) * 4 + sub // 32).astype(F32)
    first = jnp.where((tile == dest) & (rank == 0.0), 1.0, 0.0)
    second = jnp.where((tile == dest) & (rank == 1.0), 1.0, 0.0)
    chosen = jnp.concatenate([first, second], axis=1).astype(BF16)
    ordered = sum(
        lax.dot_general(chosen, part, (((1,), (1,)), ((), ())), preferred_element_type=F32) for part in split(pay)
    )
    for b in range(4):
        full = pltpu.roll(ordered[32 * b : 32 * b + 32], 2 * PAY, 1)
        if b > 0:
            full = full + ordered[32 * b - 32 : 32 * b]
        if b < 3:
            full = full + pltpu.roll(ordered[32 * b + 32 : 32 * b + 64], 4 * PAY, 1)
        for h in range(2):
            for y in range(4):
                for s in range(6):
                    at = (8 * y + 4 * h + s - 1) % 32
                    msg[4 * h + b, y, s] = full[at : at + 1]

    fdest = fdest_ref[...].astype(F32)
    place = 8.0 * fdest + ranks_of(fdest)
    fhot = (iota((40, 16), 0).astype(F32) == place).astype(F32)
    fpay = jnp.concatenate([fval_ref[:, 0], fval_ref[:, 1], fpos_ref[:, 0], fpos_ref[:, 1]], axis=1)
    fordered = jnp.dot(fhot, fpay, precision=lax.Precision.HIGHEST, preferred_element_type=F32)
    fsend[:, :, pl.ds(0, 512)] = fordered.reshape(5, 8, 512)
    flags = jnp.broadcast_to(jnp.sum(fhot, axis=1, keepdims=True), (40, 128))
    fsend[:, :, pl.ds(512, 128)] = flags.reshape(5, 8, 128)

    pl.semaphore_wait(barrier, 30)

    def remote(src, dst, s, r, peer):
        return pltpu.make_async_remote_copy(
            src_ref=src, dst_ref=dst, send_sem=s, recv_sem=r, device_id=peer, device_id_type=MESH
        )

    @pl.loop(1, 8)
    def _(d):
        t = (u + d) % 8
        remote(msg.at[t], mid.at[d], p1_s, p1_r, device_of(t, v)).start()

    top, bottom = pl.ds(61, 3), pl.ds(0, 3)
    low, high = pl.ds(69, 3), pl.ds(64, 3)
    wide = pl.ds(0, W)
    edge = []
    for i, (src, dst) in enumerate(((di_hbm, dx), (ve_hbm, vx), (tr_hbm, c0))):
        edge.append(remote(src.at[:, :, top], dst.at[:, pl.ds(0, LEVELS), low, wide], ns_s.at[i], ns_r.at[i], north))
        edge.append(remote(src.at[:, :, bottom], dst.at[:, pl.ds(0, LEVELS), high, wide], ns_s.at[4 + i], ns_r.at[4 + i], south))
    edge.append(remote(wet_hbm.at[:, top], wi.at[:, low], ns_s.at[3], ns_r.at[3], north))
    edge.append(remote(wet_hbm.at[:, bottom], wi.at[:, high], ns_s.at[7], ns_r.at[7], south))
    for i, peer in enumerate((east, west, north, south)):
        edge.append(remote(fsend.at[1 + i], fgot.at[i], fl_s.at[i], fl_r.at[i], peer))
    for copy in edge:
        copy.start()
    mid[0] = msg[u]

    for copy in loads:
        copy.wait()

    lane64 = iota((H, 128), 1)

    def planes_of(t):
        for q in range(20):
            n, k = q // LEVELS, q % LEVELS
            yield q, ((c0, (n, k)), (dx, (0, k)) if n == 0 else (vx, (0, k)), (dx, (1, k)) if n == 0 else (vx, (1, k)), (dx, (2, k)) if n == 0 else (wf, (k,)))[t]

    for k in range(LEVELS):
        wf[k, pl.ds(0, H), wide] = wi[k, pl.ds(0, H)].astype(F32)
    for t in range(4):
        acc = jnp.zeros((H, 128), F32)
        for q, (ref, at) in planes_of(t):
            left = ref[at + (pl.ds(0, H), pl.ds(0, 128))]
            right = ref[at + (pl.ds(0, H), pl.ds(384, 128))]
            both = pltpu.roll(jnp.where(lane64 < 3, left, right), 6 * q + 3, 1)
            acc = jnp.where(lane64 >= 6 * q, both, acc)
        packs[t] = acc
    sides = [
        remote(packs, from_w, ew_s.at[0], ew_r.at[0], east),
        remote(packs, from_e, ew_s.at[1], ew_r.at[1], west),
        remote(packs.at[:, pl.ds(56, 8)], from_sw, ew_s.at[2], ew_r.at[2], ne),
        remote(packs.at[:, pl.ds(56, 8)], from_se, ew_s.at[3], ew_r.at[3], nw),
        remote(packs.at[:, pl.ds(0, 8)], from_nw, ew_s.at[4], ew_r.at[4], se),
        remote(packs.at[:, pl.ds(0, 8)], from_ne, ew_s.at[5], ew_r.at[5], sw),
    ]
    for copy in sides:
        copy.start()

    done = remote(mid.at[pl.ds(1, 7)], mid.at[pl.ds(1, 7)], p1_s, p1_r, east)
    done.wait_send()
    done.wait_recv()

    @pl.loop(1, 16)
    def _(d):
        t = (v + d) % 16
        remote(mid.at[:, t // 4, pl.ds(t % 4, 3)], got.at[d], p2_s, p2_r, device_of(u, t)).start()

    got[0] = mid[:, v // 4, pl.ds(v % 4, 3)]

    sub8 = iota((8, EW), 0)

    def up(cur, nxt):
        n = cur.shape[1]
        return jnp.where(sub8[:, :n] == 7, pltpu.roll(nxt, 7, 0), pltpu.roll(cur, 7, 0))

    def coefficients(k, strip, a, b):
        rows = pl.ds(8 * strip, 8)
        after = pl.ds(8 * ((strip + 1) % STRIPS), 8)
        lanes = pl.ds(a, b - a)
        w = wf[k, rows, lanes]
        if b < EW:
            w_e = pltpu.roll(wf[k, rows, pl.ds(a, b - a + 128)], b - a + 127, 1)[:, : b - a]
        elif a == 0:
            w_e = pltpu.roll(w, EW - 1, 1)
        else:
            w_e = jnp.concatenate([w, wf[k, rows, pl.ds(0, 128)]], axis=1)
            w_e = pltpu.roll(w_e, b - a + 127, 1)[:, : b - a]
        w_n = up(w, wf[k, after, lanes])
        w_v = wf[k + 1, rows, lanes]
        for i, other in ((0, w_e), (1, w_n)):
            d, f, open_ = dx[i, k, rows, lanes], 0.5 * vx[i, k, rows, lanes], w * other
            dx[i, k, rows, lanes] = open_ * (d - f)
            vx[i, k, rows, lanes] = open_ * (d + f)
        dx[2, k, rows, lanes] = w * w_v * dx[2, k, rows, lanes]

    wf[LEVELS] = jnp.zeros((EH, EW), F32)
    for n in range(2):
        c0[n, LEVELS] = jnp.zeros((EH, EW), F32)
        c1[n, LEVELS] = jnp.zeros((EH, EW), F32)

    @pl.loop(0, LEVELS)
    def _(k):
        for strip in range(7):
            coefficients(k, strip, 0, 384)

    for i in range(4):
        edge[8 + i].wait()
    blocks = [fsend[0]] + [fgot[i] for i in range(4)]
    reach = {3: jnp.where(lat > 0, 1.0, 0.0), 4: jnp.where(lat < 3, 1.0, 0.0)}
    cells = iota((W, 128), 0)
    lows, fracs = [], []
    for g in range(5):
        for s in range(4):
            xpos = blocks[g][s : s + 1, 256:384] * (W - 1.0)
            lowest = jnp.clip(jnp.floor(xpos).astype(I32), 0, W - 2)
            fracs.append(xpos - lowest.astype(F32))
            hot[:, pl.ds(512 * g + 128 * s, 128)] = jnp.where(cells == lowest, 1.0, 0.0).astype(BF16)

    for copy in edge[:8] + sides:
        copy.wait()
    inside = jnp.where(iota((8, W), 0) < 4, jnp.where(lat < 3, 1, 0), jnp.where(lat > 0, 1, 0))
    for k in range(LEVELS):
        wf[k, pl.ds(H, 8), wide] = jnp.where(inside > 0, wi[k, pl.ds(H, 8)].astype(F32), 0.0)
    lane8 = iota((8, 128), 1)
    side = []
    for t in range(4):
        body = jnp.where(lane64 % 6 < 3, from_w[t], from_e[t])
        upper = jnp.where(lane8 % 6 < 3, from_nw[t], from_ne[t])
        lower = jnp.where(lane8 % 6 < 3, from_sw[t], from_se[t])
        side.append(jnp.concatenate([body, jnp.where(sub8[:, :128] < 4, upper, lower)], axis=0))

    done = remote(got.at[pl.ds(1, 15)], got.at[pl.ds(1, 15)], p2_s, p2_r, east)
    done.wait_send()
    done.wait_recv()

    cols_of, rows_of, vals, valsT = {}, {}, {}, {}
    for g in range(3):
        vals[g] = got[:, :, g].reshape(128, 128)
        valsT[g] = vals[g].T
        cols_of[g] = (vals[g].astype(I32) - 1) & (W - 1)
        rows_of[g] = (valsT[g].astype(I32) - 1) >> 9

    def base(dlat, slot):
        return PAY * (2 * (dlat + 1) + slot)

    wide_lane = iota((128, W), 1)

    def column_hot(g, dlat):
        parts = []
        for slot in range(2):
            at = base(dlat, slot) + 20
            parts.append(jnp.where(wide_lane == cols_of[g][:, at : at + 1], 1.0, 0.0))
        return jnp.concatenate(parts, axis=0).astype(BF16)

    def row_ids(g, dlat):
        ats = [base(dlat, slot) + 20 for slot in range(2)]
        return jnp.concatenate([rows_of[g][at : at + 1] for at in ats], axis=1)

    def value_row(g, dlat, c):
        ats = [base(dlat, slot) + c for slot in range(2)]
        return jnp.concatenate([valsT[g][at : at + 1] for at in ats], axis=1)

    own = jnp.where(iota((H, 256), 0) == row_ids(1, 0), 1.0, 0.0)
    for c in range(20):
        value = value_row(1, 0, c)
        value_hi = value.astype(BF16).astype(F32)
        amat[pl.ds(H * c, H), pl.ds(0, 256)] = (own * value_hi).astype(BF16)
        amat[pl.ds(H * c, H), pl.ds(256, 256)] = (own * (value - value_hi)).astype(BF16)
    amat[pl.ds(H * 20, H), pl.ds(0, 256)] = own.astype(BF16)
    amat[pl.ds(H * 20, H), pl.ds(256, 256)] = jnp.zeros((H, 256), BF16)
    onto = column_hot(1, 0)
    onto = jnp.concatenate([onto, onto], axis=0)
    added = jnp.dot(amat[...], onto, preferred_element_type=F32)
    keep = 1.0 - 0.5 * added[H * 20 :]
    for c in range(20):
        at = (c // LEVELS, c % LEVELS, pl.ds(0, H), wide)
        c0[at] = c0[at] * keep + added[H * c : H * c + H]

    sub256 = iota((8, 256), 0)
    north_ids, south_ids = row_ids(1, 1), row_ids(1, -1)
    hits = [
        jnp.where((sub256 == north_ids) & (sub256 < 4), 1.0, 0.0),
        jnp.where((sub256 + 56 == south_ids) & (sub256 >= 4), 1.0, 0.0),
    ]
    hits = jnp.concatenate(hits, axis=1)
    parts = []
    for c in range(20):
        parts.append(hits * jnp.concatenate([value_row(1, 1, c), value_row(1, -1, c)], axis=1))
    parts.append(hits)
    parts.append(jnp.zeros_like(hits))
    near = jnp.concatenate(parts, axis=0)
    onto = jnp.concatenate([column_hot(1, 1), column_hot(1, -1)], axis=0)
    added = sum(jnp.dot(part, onto, preferred_element_type=F32) for part in split(near))
    keep = 1.0 - 0.5 * added[160:168]
    for c in range(20):
        at = (c // LEVELS, c % LEVELS, pl.ds(H, 8), wide)
        c0[at] = c0[at] * keep + added[8 * c : 8 * c + 8]

    spread_from, spread_to = iota((128, 6 * 128), 0), iota((128, 6 * 128), 1)
    spread_lane = spread_to % 128
    spread = (spread_from == PAY * (spread_to // 128) + spread_lane // 6) & (spread_lane < 120)
    spread = jnp.where(spread, 1.0, 0.0).astype(BF16)
    sub72 = iota((EH, 128), 0)
    lane128 = iota((128, 128), 1)
    within = lane128 % 6
    pick, hi_parts, lo_parts, ones = [], [], [], []
    for g in (0, 2):
        grown = [jnp.dot(part, spread, preferred_element_type=F32) for part in split(vals[g])]
        target = jnp.where(within < 3, 509 + within, -1) if g == 0 else jnp.where(within >= 3, within - 3, -1)
        target = jnp.where(lane128 < 120, target, -1)
        for dlat in (-1, 0, 1):
            for slot in range(2):
                at = base(dlat, slot) + 20
                ids = rows_of[g][at : at + 1]
                if dlat == 1:
                    ids = jnp.where((ids >= 0) & (ids < 4), ids + H, -1)
                elif dlat == -1:
                    ids = jnp.where(ids >= 60, ids + 8, -1)
                pick.append(jnp.where(sub72 == ids, 1.0, 0.0))
                match = jnp.where(cols_of[g][:, at : at + 1] == target, 1.0, 0.0)
                block = 2 * (dlat + 1) + slot
                hi_parts.append(match * grown[0][:, 128 * block : 128 * block + 128])
                lo_parts.append(match * grown[1][:, 128 * block : 128 * block + 128])
                ones.append(match)
    pick = jnp.concatenate(pick, axis=1).astype(BF16)
    onto = jnp.concatenate([jnp.concatenate(p, axis=0).astype(BF16) for p in (hi_parts, lo_parts, ones)], axis=1)
    added = jnp.dot(pick, onto, preferred_element_type=F32)
    side[0] = side[0] * (1.0 - 0.5 * added[:, 256:384]) + added[:, 0:128] + added[:, 128:256]

    for t in range(4):
        for q, (ref, at) in planes_of(t):
            values = pltpu.roll(side[t], (128 - 6 * q - 3) % 128, 1)
            if ref is wf:
                edge_rows = jnp.where(inside[:, :128] > 0, values[H:], 0.0)
                values = jnp.concatenate([values[:H], edge_rows], axis=0)
            ref[at + (slice(None), pl.ds(W, 128))] = values

    @pl.loop(0, LEVELS)
    def _(k):
        for strip in range(7):
            coefficients(k, strip, 384, EW)
        for strip in (7, 8):
            coefficients(k, strip, 0, EW)

    def step(src, dst, last):
        vbuf[...] = jnp.zeros((2, EH, EW), F32)

        @pl.loop(0, LEVELS)
        def _(k):
            def strip_of(n, i):
                return src[n, k, pl.ds(8 * (i % STRIPS), 8), :]

            def face_n(i, cur, cur_n):
                rows = pl.ds(8 * i, 8)
                return dx[1, k, rows, :] * cur_n - vx[1, k, rows, :] * cur

            cur, turned, below = {}, {}, {}
            for n in range(2):
                tail, head = strip_of(n, 8), strip_of(n, 0)
                turned[n] = pltpu.roll(head, 7, 0)
                tail_n = jnp.where(sub8 == 7, turned[n], pltpu.roll(tail, 7, 0))
                below[n] = pltpu.roll(face_n(8, tail, tail_n), 1, 0)
                cur[n] = head
            for i in range(8 if last else STRIPS):
                rows = pl.ds(8 * i, 8)
                for n in range(2):
                    here = cur[n]
                    after = strip_of(n, i + 1)
                    after_turned = pltpu.roll(after, 7, 0)
                    flux_n = face_n(i, here, jnp.where(sub8 == 7, after_turned, turned[n]))
                    flux_turned = pltpu.roll(flux_n, 1, 0)
                    new = here + (flux_n - jnp.where(sub8 == 0, below[n], flux_turned))
                    flux_e = dx[0, k, rows, :] * pltpu.roll(here, EW - 1, 1) - vx[0, k, rows, :] * here
                    new = new + (flux_e - pltpu.roll(flux_e, 1, 1))
                    flux_v = dx[2, k, rows, :] * (src[n, k + 1, rows, :] - here)
                    new = new + (flux_v - vbuf[n, rows, :])
                    vbuf[n, rows, :] = flux_v
                    if last:
                        dst[n, k, rows, :] = new[:, :W]
                    else:
                        dst[n, k, rows, :] = new
                    cur[n], turned[n], below[n] = after, after_turned, flux_turned

    step(c0, c1, False)
    step(c1, c0, False)
    step(c0, out_ref, True)

    plane = jnp.concatenate([out_ref[0, 0], out_ref[1, 0]], axis=0)
    nexts = pltpu.roll(plane, W - 1, 1)
    lhs = jnp.concatenate(list(split(plane)) + list(split(nexts)), axis=0)
    line = iota((H, 128), 0).astype(F32)
    for g in range(5):
        res = jnp.dot(lhs, hot[:, pl.ds(512 * g, 512)], preferred_element_type=F32)
        for s in range(4):
            part = res[:, 128 * s : 128 * s + 128]
            frac = fracs[4 * g + s]
            along = (1.0 - frac) * (part[0:128] + part[128:256]) + frac * (part[256:384] + part[384:512])
            ypos = blocks[g][s : s + 1, 384:512] * (H - 1.0)
            tent = jnp.maximum(0.0, 1.0 - jnp.abs(ypos - line))
            flag = blocks[g][s : s + 1, 512:640]
            for n in range(2):
                sample = jnp.sum(along[H * n : H * n + H] * tent, axis=0, keepdims=True)
                value = flag * (0.5 * blocks[g][s : s + 1, 128 * n : 128 * n + 128] + 0.5 * sample)
                if g in reach:
                    value = reach[g] * value
                fout_ref[4 * g + s, pl.ds(n, 1), :] = value


def shards(tracers, diffusivity, velocity, wet_mask, argo_rows, argo_dest, argo_cols, argo_count, float_values, float_pos, float_dest):
    vmem = pl.BlockSpec(memory_space=pltpu.VMEM)
    hbm = pl.BlockSpec(memory_space=pl.ANY)
    smem = pl.BlockSpec(memory_space=pltpu.SMEM)
    dma, scratch = pltpu.SemaphoreType.DMA, pltpu.VMEM
    return pl.pallas_call(
        kernel,
        out_shape=(
            jax.ShapeDtypeStruct(tracers.shape, F32),
            jax.ShapeDtypeStruct((20, 2, 128), F32),
        ),
        in_specs=[hbm] * 4 + [vmem, vmem, vmem, smem, vmem, vmem, vmem],
        out_specs=(vmem, vmem),
        scratch_shapes=[
            scratch((2, LEVELS + 1, EH, EW), F32),
            scratch((2, LEVELS + 1, EH, EW), F32),
            scratch((3, LEVELS, EH, EW), F32),
            scratch((2, LEVELS, EH, EW), F32),
            scratch((LEVELS, EH, W), I32),
            scratch((LEVELS + 1, EH, EW), F32),
            scratch((2, EH, EW), F32),
            scratch((4, H, 128), F32),
            scratch((4, H, 128), F32),
            scratch((4, H, 128), F32),
            scratch((4, 8, 128), F32),
            scratch((4, 8, 128), F32),
            scratch((4, 8, 128), F32),
            scratch((4, 8, 128), F32),
            scratch((8, 4, 6, 1, 128), F32),
            scratch((8, 4, 6, 1, 128), F32),
            scratch((16, 8, 3, 1, 128), F32),
            scratch((5, 8, 640), F32),
            scratch((4, 8, 640), F32),
            scratch((H * 21, 512), BF16),
            scratch((W, 2560), BF16),
            dma((4,)), dma, dma, dma, dma, dma((8,)), dma((8,)), dma((6,)), dma((6,)), dma((4,)), dma((4,)),
        ],
        compiler_params=pltpu.CompilerParams(
            collective_id=1, has_side_effects=True, vmem_limit_bytes=60 * 1024 * 1024
        ),
    )(
        tracers, diffusivity, velocity, wet_mask, argo_rows, argo_dest.reshape(1, -1), argo_cols.reshape(1, -1),
        argo_count, float_values, float_pos, float_dest.reshape(1, -1),
    )


def solution(mesh):
    grid4, grid3 = P(None, None, "lat", "lon"), P(None, "lat", "lon")
    tiles = ("lon", "lat")
    return jax.shard_map(
        shards,
        mesh=mesh,
        in_specs=(
            grid4, grid4, grid4, grid3, P(tiles, None), P(tiles, None), P(tiles), P(tiles),
            P(tiles, None, None), P(tiles, None, None), P(tiles, None),
        ),
        out_specs=(grid4, P(tiles, None, None)),
        check_vma=False,
    )
```

profile of v0, /device:TPU:1, one launch (start us, length us, event | category | flops | bytes accessed | tf_op | source)
XLA Modules:
  0.0 63.7 jit_solution(9788706064369010848)
XLA Ops:
  1.3 58.2 %shard_map.122 = (f32[2,10,64,512]{3,2,1,0:T(8,128)}, f32[20,2,128]{2,1,0:T(2,128)}) custom-call(f32[2,10,64,512]{3,2,1,0:T(8,128)} %tr_hbm.1, f32[3,10,64,512]{3,2,1,0:T(8,128)} %di_hbm.1, f32[2,10,64,512]{3,2,1,0:T(8,128)} %ve_hbm.1, s32[10,64,512]{2,1,0:T(8,128)} %wet_hbm.1, f32[128,128]{1,0:T(8,128)} %rows_ref.1, s32[1,128]{1,0:T(1,128)} %bitcast.3, ...), custom_call_target="tpu_custom_call" | custom-call | tf_op jit(solution)/shard_map/pallas_call | solution.py:445
  59.5 0.0 copy-start
  59.5 3.6 %copy.16 = f32[2,10,64,512]{3,2,1,0:T(8,128)} copy(f32[2,10,64,512]{3,2,1,0:T(8,128)} %get-tuple-element.4) | data formatting | bytes 5242880
  63.1 0.0 copy-done
  63.1 0.6 copy.17
Async XLA Ops:
  59.5 3.6 %copy-start = (f32[20,2,128]{2,1,0:T(2,128)S(1)}, f32[20,2,128]{2,1,0:T(2,128)}, u32[]{:S(2)}) copy-start(f32[20,2,128]{2,1,0:T(2,128)} %get-tuple-element.5) | copy-start | bytes 61444
where the time goes:
time: 63.9 us; the launch traced here: 63.7 us
  Pallas kernels  58.2 us (91%)
  local copies, waits for them, and re-layouts  4.19 us (7%)
  between operations  1.3 us (2%)
    pallas_call x1, Pallas kernels, shards(): pl.pallas_call(kernel, out_shape=(jax.ShapeDtypeStruct(tracers.shape, F32...  58.2 us
    unnamed x4, local copies, waits for them, and re-layouts  4.19 us

commit v1 on v0

--- a/solution.py
+++ b/solution.py
@@ -13,6 +13,7 @@
 LEVELS, H, W = 10, 64, 512
 EH, EW = 72, 640
 STRIPS = EH // 8
+GAP = 3
 PAY = 21
 
 
@@ -52,8 +53,8 @@
     tr_hbm, di_hbm, ve_hbm, wet_hbm, rows_ref, dest_ref, cols_ref, count_ref, fval_ref, fpos_ref, fdest_ref,
     out_ref, fout_ref,
     c0, c1, dx, vx, wi, wf, vbuf, packs, from_w, from_e, from_nw, from_sw, from_ne, from_se,
-    msg, mid, got, fsend, fgot, amat, hot,
-    load_sem, p1_s, p1_r, p2_s, p2_r, ns_s, ns_r, ew_s, ew_r, fl_s, fl_r,
+    msg, mid, got, fsend, fgot, amat, hot, spread,
+    load_sem, p1_s, p1_r, p2_s, p2_r, ns_s, ns_r, ew_s, ew_r, fl_s, fl_r, row_s, row_r,
 ):
     lon, lat, u, v = places()
     east, west = ((lon + 1) % 32, lat), ((lon + 31) % 32, lat)
@@ -109,16 +110,13 @@
         lax.dot_general(chosen, part, (((1,), (1,)), ((), ())), preferred_element_type=F32) for part in split(pay)
     )
     for b in range(4):
-        full = pltpu.roll(ordered[32 * b : 32 * b + 32], 2 * PAY, 1)
-        if b > 0:
-            full = full + ordered[32 * b - 32 : 32 * b]
-        if b < 3:
-            full = full + pltpu.roll(ordered[32 * b + 32 : 32 * b + 64], 4 * PAY, 1)
+        mine = ordered[32 * b : 32 * b + 32]
+        full = pltpu.roll(mine, 1, 0) + pltpu.roll(mine, 2 * PAY, 1) + pltpu.roll(pltpu.roll(mine, 31, 0), 4 * PAY, 1)
         for h in range(2):
             for y in range(4):
-                for s in range(6):
-                    at = (8 * y + 4 * h + s - 1) % 32
-                    msg[4 * h + b, y, s] = full[at : at + 1]
+                for z in range(4):
+                    at = 8 * y + 4 * h + z
+                    msg[4 * h + b, y, z] = full[at : at + 1]
 
     fdest = fdest_ref[...].astype(F32)
     place = 8.0 * fdest + ranks_of(fdest)
@@ -141,15 +139,15 @@
         t = (u + d) % 8
         remote(msg.at[t], mid.at[d], p1_s, p1_r, device_of(t, v)).start()
 
-    top, bottom = pl.ds(61, 3), pl.ds(0, 3)
-    low, high = pl.ds(69, 3), pl.ds(64, 3)
+    top, bottom = pl.ds(H - 1, 1), pl.ds(0, 1)
+    low, high = pl.ds(EH - 1, 1), pl.ds(H, 1)
     wide = pl.ds(0, W)
-    edge = []
-    for i, (src, dst) in enumerate(((di_hbm, dx), (ve_hbm, vx), (tr_hbm, c0))):
-        edge.append(remote(src.at[:, :, top], dst.at[:, pl.ds(0, LEVELS), low, wide], ns_s.at[i], ns_r.at[i], north))
-        edge.append(remote(src.at[:, :, bottom], dst.at[:, pl.ds(0, LEVELS), high, wide], ns_s.at[4 + i], ns_r.at[4 + i], south))
-    edge.append(remote(wet_hbm.at[:, top], wi.at[:, low], ns_s.at[3], ns_r.at[3], north))
-    edge.append(remote(wet_hbm.at[:, bottom], wi.at[:, high], ns_s.at[7], ns_r.at[7], south))
+    edge = [
+        remote(di_hbm.at[1, :, top], dx.at[1, :, low, wide], ns_s.at[0], ns_r.at[0], north),
+        remote(ve_hbm.at[1, :, top], vx.at[1, :, low, wide], ns_s.at[1], ns_r.at[1], north),
+        remote(wet_hbm.at[:, top], wi.at[:, low], ns_s.at[2], ns_r.at[2], north),
+        remote(wet_hbm.at[:, bottom], wi.at[:, high], ns_s.at[3], ns_r.at[3], south),
+    ]
     for i, peer in enumerate((east, west, north, south)):
         edge.append(remote(fsend.at[1 + i], fgot.at[i], fl_s.at[i], fl_r.at[i], peer))
     for copy in edge:
@@ -194,9 +192,9 @@
     @pl.loop(1, 16)
     def _(d):
         t = (v + d) % 16
-        remote(mid.at[:, t // 4, pl.ds(t % 4, 3)], got.at[d], p2_s, p2_r, device_of(u, t)).start()
-
-    got[0] = mid[:, v // 4, pl.ds(v % 4, 3)]
+        remote(mid.at[:, t // 4, t % 4], got.at[d], p2_s, p2_r, device_of(u, t)).start()
+
+    got[0] = mid[:, v // 4, v % 4]
 
     sub8 = iota((8, EW), 0)
 
@@ -219,10 +217,13 @@
         w_n = up(w, wf[k, after, lanes])
         w_v = wf[k + 1, rows, lanes]
         for i, other in ((0, w_e), (1, w_n)):
+            if strip == 8 and i == 0:
+                continue
             d, f, open_ = dx[i, k, rows, lanes], 0.5 * vx[i, k, rows, lanes], w * other
             dx[i, k, rows, lanes] = open_ * (d - f)
             vx[i, k, rows, lanes] = open_ * (d + f)
-        dx[2, k, rows, lanes] = w * w_v * dx[2, k, rows, lanes]
+        if strip < 8:
+            dx[2, k, rows, lanes] = w * w_v * dx[2, k, rows, lanes]
 
     wf[LEVELS] = jnp.zeros((EH, EW), F32)
     for n in range(2):
@@ -234,8 +235,19 @@
         for strip in range(7):
             coefficients(k, strip, 0, 384)
 
+    spread_lane = iota((128, 128), 1)
+    within = spread_lane % 6
+    picked = spread_lane // 6
+    inner = spread_lane < 120
+    for b, start in enumerate((0, PAY, 4 * PAY, 5 * PAY)):
+        hit = (iota((128, 128), 0) == start + picked) & inner
+        spread[:, pl.ds(128 * b, 128)] = jnp.where(hit, 1.0, 0.0).astype(BF16)
+    targets = (
+        jnp.where((within < 3) & inner, 509 + within, -1), jnp.where((within >= 3) & inner, within - 3, -1)
+    )
+
     for i in range(4):
-        edge[8 + i].wait()
+        edge[4 + i].wait()
     blocks = [fsend[0]] + [fgot[i] for i in range(4)]
     reach = {3: jnp.where(lat > 0, 1.0, 0.0), 4: jnp.where(lat < 3, 1.0, 0.0)}
     cells = iota((W, 128), 0)
@@ -247,7 +259,7 @@
             fracs.append(xpos - lowest.astype(F32))
             hot[:, pl.ds(512 * g + 128 * s, 128)] = jnp.where(cells == lowest, 1.0, 0.0).astype(BF16)
 
-    for copy in edge[:8] + sides:
+    for copy in edge[:4] + sides:
         copy.wait()
     inside = jnp.where(iota((8, W), 0) < 4, jnp.where(lat < 3, 1, 0), jnp.where(lat > 0, 1, 0))
     for k in range(LEVELS):
@@ -260,161 +272,159 @@
         lower = jnp.where(lane8 % 6 < 3, from_sw[t], from_se[t])
         side.append(jnp.concatenate([body, jnp.where(sub8[:, :128] < 4, upper, lower)], axis=0))
 
+    def unpack(t, q, ref, at):
+        values = pltpu.roll(side[t], (128 - 6 * q - 3) % 128, 1)
+        if ref is wf:
+            edge_rows = jnp.where(inside[:, :128] > 0, values[H:], 0.0)
+            values = jnp.concatenate([values[:H], edge_rows], axis=0)
+        return ref, at, values
+
+    def unpack_all(blocks_of):
+        held = []
+        for t in blocks_of:
+            for q, (ref, at) in planes_of(t):
+                held.append(unpack(t, q, ref, at))
+                if len(held) > 3:
+                    ref, at, values = held.pop(0)
+                    ref[at + (pl.ds(0, values.shape[0]), pl.ds(W, 128))] = values
+        for ref, at, values in held:
+            ref[at + (pl.ds(0, values.shape[0]), pl.ds(W, 128))] = values
+
+    unpack_all((1, 2, 3))
+
+    @pl.loop(0, LEVELS)
+    def _(k):
+        for strip in range(7):
+            coefficients(k, strip, 384, EW)
+        coefficients(k, 7, 0, EW)
+        coefficients(k, 8, 0, EW)
+
     done = remote(got.at[pl.ds(1, 15)], got.at[pl.ds(1, 15)], p2_s, p2_r, east)
     done.wait_send()
     done.wait_recv()
 
-    cols_of, rows_of, vals, valsT = {}, {}, {}, {}
-    for g in range(3):
-        vals[g] = got[:, :, g].reshape(128, 128)
-        valsT[g] = vals[g].T
-        cols_of[g] = (vals[g].astype(I32) - 1) & (W - 1)
-        rows_of[g] = (valsT[g].astype(I32) - 1) >> 9
-
-    def base(dlat, slot):
-        return PAY * (2 * (dlat + 1) + slot)
+    rims = {}
+
+    def exchange(ref, number):
+        def rim(a, b, i, peer):
+            at = [ref.at[:, pl.ds(0, LEVELS), pl.ds(r, 1)] for r in (a, b)]
+            return remote(at[0], at[1], row_s.at[2 * number + i], row_r.at[2 * number + i], peer)
+
+        rims[number] = rim(H - 1, EH - 1, 0, north), rim(0, H, 1, south)
+        for copy in rims[number]:
+            copy.start()
+
+    vals = got[...].reshape(128, 128)
+    valsT = vals.T
+    cols = (vals.astype(I32) - 1) & (W - 1)
+    rowsT = (valsT.astype(I32) - 1) >> 9
+
+    grown = [jnp.dot(part, spread[...], preferred_element_type=F32) for part in split(vals)]
+    sub64 = iota((H, 128), 0)
+    pick, hi_parts, lo_parts, ones = [], [], [], []
+    for b, start in enumerate((0, PAY, 4 * PAY, 5 * PAY)):
+        at = start + PAY - 1
+        pick.append(jnp.where(sub64 == rowsT[at : at + 1], 1.0, 0.0))
+        match = jnp.where(cols[:, at : at + 1] == targets[b // 2], 1.0, 0.0)
+        hi_parts.append(match * grown[0][:, 128 * b : 128 * b + 128])
+        lo_parts.append(match * grown[1][:, 128 * b : 128 * b + 128])
+        ones.append(match)
+    pick = jnp.concatenate(pick, axis=1).astype(BF16)
+    onto = jnp.concatenate([jnp.concatenate(p, axis=0).astype(BF16) for p in (hi_parts, lo_parts, ones)], axis=1)
+    beside = jnp.dot(pick, onto, preferred_element_type=F32)
 
     wide_lane = iota((128, W), 1)
-
-    def column_hot(g, dlat):
-        parts = []
-        for slot in range(2):
-            at = base(dlat, slot) + 20
-            parts.append(jnp.where(wide_lane == cols_of[g][:, at : at + 1], 1.0, 0.0))
-        return jnp.concatenate(parts, axis=0).astype(BF16)
-
-    def row_ids(g, dlat):
-        ats = [base(dlat, slot) + 20 for slot in range(2)]
-        return jnp.concatenate([rows_of[g][at : at + 1] for at in ats], axis=1)
-
-    def value_row(g, dlat, c):
-        ats = [base(dlat, slot) + c for slot in range(2)]
-        return jnp.concatenate([valsT[g][at : at + 1] for at in ats], axis=1)
-
-    own = jnp.where(iota((H, 256), 0) == row_ids(1, 0), 1.0, 0.0)
+    slots = (2 * PAY, 3 * PAY)
+    own_rows = jnp.concatenate([rowsT[b + PAY - 1 : b + PAY] for b in slots], axis=1)
+    own = jnp.where(iota((H, 256), 0) == own_rows, 1.0, 0.0)
     for c in range(20):
-        value = value_row(1, 0, c)
+        value = jnp.concatenate([valsT[b + c : b + c + 1] for b in slots], axis=1)
         value_hi = value.astype(BF16).astype(F32)
         amat[pl.ds(H * c, H), pl.ds(0, 256)] = (own * value_hi).astype(BF16)
         amat[pl.ds(H * c, H), pl.ds(256, 256)] = (own * (value - value_hi)).astype(BF16)
     amat[pl.ds(H * 20, H), pl.ds(0, 256)] = own.astype(BF16)
     amat[pl.ds(H * 20, H), pl.ds(256, 256)] = jnp.zeros((H, 256), BF16)
-    onto = column_hot(1, 0)
-    onto = jnp.concatenate([onto, onto], axis=0)
+    onto = [jnp.where(wide_lane == cols[:, b + PAY - 1 : b + PAY], 1.0, 0.0) for b in slots]
+    onto = jnp.concatenate(onto + onto, axis=0).astype(BF16)
     added = jnp.dot(amat[...], onto, preferred_element_type=F32)
     keep = 1.0 - 0.5 * added[H * 20 :]
     for c in range(20):
         at = (c // LEVELS, c % LEVELS, pl.ds(0, H), wide)
         c0[at] = c0[at] * keep + added[H * c : H * c + H]
-
-    sub256 = iota((8, 256), 0)
-    north_ids, south_ids = row_ids(1, 1), row_ids(1, -1)
-    hits = [
-        jnp.where((sub256 == north_ids) & (sub256 < 4), 1.0, 0.0),
-        jnp.where((sub256 + 56 == south_ids) & (sub256 >= 4), 1.0, 0.0),
-    ]
-    hits = jnp.concatenate(hits, axis=1)
-    parts = []
-    for c in range(20):
-        parts.append(hits * jnp.concatenate([value_row(1, 1, c), value_row(1, -1, c)], axis=1))
-    parts.append(hits)
-    parts.append(jnp.zeros_like(hits))
-    near = jnp.concatenate(parts, axis=0)
-    onto = jnp.concatenate([column_hot(1, 1), column_hot(1, -1)], axis=0)
-    added = sum(jnp.dot(part, onto, preferred_element_type=F32) for part in split(near))
-    keep = 1.0 - 0.5 * added[160:168]
-    for c in range(20):
-        at = (c // LEVELS, c % LEVELS, pl.ds(H, 8), wide)
-        c0[at] = c0[at] * keep + added[8 * c : 8 * c + 8]
-
-    spread_from, spread_to = iota((128, 6 * 128), 0), iota((128, 6 * 128), 1)
-    spread_lane = spread_to % 128
-    spread = (spread_from == PAY * (spread_to // 128) + spread_lane // 6) & (spread_lane < 120)
-    spread = jnp.where(spread, 1.0, 0.0).astype(BF16)
-    sub72 = iota((EH, 128), 0)
-    lane128 = iota((128, 128), 1)
-    within = lane128 % 6
-    pick, hi_parts, lo_parts, ones = [], [], [], []
-    for g in (0, 2):
-        grown = [jnp.dot(part, spread, preferred_element_type=F32) for part in split(vals[g])]
-        target = jnp.where(within < 3, 509 + within, -1) if g == 0 else jnp.where(within >= 3, within - 3, -1)
-        target = jnp.where(lane128 < 120, target, -1)
-        for dlat in (-1, 0, 1):
-            for slot in range(2):
-                at = base(dlat, slot) + 20
-                ids = rows_of[g][at : at + 1]
-                if dlat == 1:
-                    ids = jnp.where((ids >= 0) & (ids < 4), ids + H, -1)
-                elif dlat == -1:
-                    ids = jnp.where(ids >= 60, ids + 8, -1)
-                pick.append(jnp.where(sub72 == ids, 1.0, 0.0))
-                match = jnp.where(cols_of[g][:, at : at + 1] == target, 1.0, 0.0)
-                block = 2 * (dlat + 1) + slot
-                hi_parts.append(match * grown[0][:, 128 * block : 128 * block + 128])
-                lo_parts.append(match * grown[1][:, 128 * block : 128 * block + 128])
-                ones.append(match)
-    pick = jnp.concatenate(pick, axis=1).astype(BF16)
-    onto = jnp.concatenate([jnp.concatenate(p, axis=0).astype(BF16) for p in (hi_parts, lo_parts, ones)], axis=1)
-    added = jnp.dot(pick, onto, preferred_element_type=F32)
-    side[0] = side[0] * (1.0 - 0.5 * added[:, 256:384]) + added[:, 0:128] + added[:, 128:256]
-
-    for t in range(4):
-        for q, (ref, at) in planes_of(t):
-            values = pltpu.roll(side[t], (128 - 6 * q - 3) % 128, 1)
-            if ref is wf:
-                edge_rows = jnp.where(inside[:, :128] > 0, values[H:], 0.0)
-                values = jnp.concatenate([values[:H], edge_rows], axis=0)
-            ref[at + (slice(None), pl.ds(W, 128))] = values
-
-    @pl.loop(0, LEVELS)
-    def _(k):
-        for strip in range(7):
-            coefficients(k, strip, 384, EW)
-        for strip in (7, 8):
-            coefficients(k, strip, 0, EW)
-
-    def step(src, dst, last):
-        vbuf[...] = jnp.zeros((2, EH, EW), F32)
-
+    body = side[0][:H]
+    side[0] = body * (1.0 - 0.5 * beside[:, 256:384]) + beside[:, 0:128] + beside[:, 128:256]
+
+    unpack_all((0,))
+    exchange(c0, 0)
+
+    tiles = EW // 128
+    first_lane, last_lane = iota((8, 128), 1) == 0, iota((8, 128), 1) == 127
+    first_row, last_row = iota((8, 128), 0) == 0, iota((8, 128), 0) == 7
+
+    def sweep(src, dst, last, starts):
         @pl.loop(0, LEVELS)
         def _(k):
-            def strip_of(n, i):
-                return src[n, k, pl.ds(8 * (i % STRIPS), 8), :]
-
-            def face_n(i, cur, cur_n):
+            def load(ref, at, i):
+                return [ref[at + (pl.ds(8 * (i % STRIPS), 8), pl.ds(128 * j, 128))] for j in range(tiles)]
+
+            started, fluxes, turned, below = {}, {}, {}, {}
+
+            def start(i, n):
+                here = load(src, (n, k), i)
+                started[i, n] = here, [pltpu.roll(x, 127, 1) for x in here]
+
+            def face(i, n):
+                here, moved = started.pop((i, n))
+                east_of = [jnp.where(last_lane, moved[(j + 1) % tiles], moved[j]) for j in range(tiles)]
+                flux = [
+                    a * x - b * y for a, b, x, y in zip(load(dx, (0, k), i), load(vx, (0, k), i), east_of, here)
+                ]
+                fluxes[i, n] = here, flux, [pltpu.roll(x, 1, 1) for x in flux]
+
+            def north_flux(i, here, above):
+                return [a * x - b * y for a, b, x, y in zip(load(dx, (1, k), i), load(vx, (1, k), i), above, here)]
+
+            def finish(i, n):
+                here, flux, moved = fluxes.pop((i, n))
+                lifted = [pltpu.roll(x, 7, 0) for x in load(src, (n, k), i + 1)]
+                above = [jnp.where(last_row, a, b) for a, b in zip(lifted, turned[i, n])]
+                flux_n = north_flux(i, here, above)
+                dropped = [pltpu.roll(x, 1, 0) for x in flux_n]
+                higher = load(src, (n, k + 1), i)
+                flux_v = [c * (x - y) for c, x, y in zip(load(dx, (2, k), i), higher, here)]
+                flux_u = load(vbuf, (n,), i)
                 rows = pl.ds(8 * i, 8)
-                return dx[1, k, rows, :] * cur_n - vx[1, k, rows, :] * cur
-
-            cur, turned, below = {}, {}, {}
-            for n in range(2):
-                tail, head = strip_of(n, 8), strip_of(n, 0)
-                turned[n] = pltpu.roll(head, 7, 0)
-                tail_n = jnp.where(sub8 == 7, turned[n], pltpu.roll(tail, 7, 0))
-                below[n] = pltpu.roll(face_n(8, tail, tail_n), 1, 0)
-                cur[n] = head
-            for i in range(8 if last else STRIPS):
-                rows = pl.ds(8 * i, 8)
+                for j in range(tiles):
+                    vbuf[n, rows, pl.ds(128 * j, 128)] = flux_v[j]
+                    if last and j == tiles - 1:
+                        continue
+                    new = here[j] + (flux_n[j] - jnp.where(first_row, below[i, n][j], dropped[j]))
+                    new = new + (flux[j] - jnp.where(first_lane, moved[j - 1], moved[j])) + (flux_v[j] - flux_u[j])
+                    dst[n, k, rows, pl.ds(128 * j, 128)] = new
+                turned[i + 1, n], below[i + 1, n] = lifted, dropped
+
+            chunks = []
+            for first, count in starts:
                 for n in range(2):
-                    here = cur[n]
-                    after = strip_of(n, i + 1)
-                    after_turned = pltpu.roll(after, 7, 0)
-                    flux_n = face_n(i, here, jnp.where(sub8 == 7, after_turned, turned[n]))
-                    flux_turned = pltpu.roll(flux_n, 1, 0)
-                    new = here + (flux_n - jnp.where(sub8 == 0, below[n], flux_turned))
-                    flux_e = dx[0, k, rows, :] * pltpu.roll(here, EW - 1, 1) - vx[0, k, rows, :] * here
-                    new = new + (flux_e - pltpu.roll(flux_e, 1, 1))
-                    flux_v = dx[2, k, rows, :] * (src[n, k + 1, rows, :] - here)
-                    new = new + (flux_v - vbuf[n, rows, :])
-                    vbuf[n, rows, :] = flux_v
-                    if last:
-                        dst[n, k, rows, :] = new[:, :W]
-                    else:
-                        dst[n, k, rows, :] = new
-                    cur[n], turned[n], below[n] = after, after_turned, flux_turned
-
-    step(c0, c1, False)
-    step(c1, c0, False)
-    step(c0, out_ref, True)
+                    prev = (first - 1) % STRIPS
+                    tail, head = load(src, (n, k), prev), load(src, (n, k), first)
+                    turned[first, n] = [pltpu.roll(x, 7, 0) for x in head]
+                    above = [jnp.where(last_row, a, pltpu.roll(b, 7, 0)) for a, b in zip(turned[first, n], tail)]
+                    below[first, n] = [pltpu.roll(x, 1, 0) for x in north_flux(prev, tail, above)]
+                chunks += [(first + i, n) for i in range(count) for n in range(2)]
+            for at in range(len(chunks) + 2 * GAP):
+                for stage, work in enumerate((start, face, finish)):
+                    if 0 <= at - stage * GAP < len(chunks):
+                        work(*chunks[at - stage * GAP])
+
+    for number, (src, dst) in enumerate(((c0, c1), (c1, c0), (c0, out_ref))):
+        vbuf[...] = jnp.zeros((2, EH, EW), F32)
+        sweep(src, dst, number == 2, [(1, 6)])
+        for copy in rims[number]:
+            copy.wait()
+        sweep(src, dst, number == 2, [(7, 1), (0, 1)])
+        if number < 2:
+            exchange(dst, number + 1)
 
     plane = jnp.concatenate([out_ref[0, 0], out_ref[1, 0]], axis=0)
     nexts = pltpu.roll(plane, W - 1, 1)
@@ -465,14 +475,16 @@
             scratch((4, 8, 128), F32),
             scratch((4, 8, 128), F32),
             scratch((4, 8, 128), F32),
-            scratch((8, 4, 6, 1, 128), F32),
-            scratch((8, 4, 6, 1, 128), F32),
-            scratch((16, 8, 3, 1, 128), F32),
+            scratch((8, 4, 4, 1, 128), F32),
+            scratch((8, 4, 4, 1, 128), F32),
+            scratch((16, 8, 1, 128), F32),
             scratch((5, 8, 640), F32),
             scratch((4, 8, 640), F32),
             scratch((H * 21, 512), BF16),
             scratch((W, 2560), BF16),
-            dma((4,)), dma, dma, dma, dma, dma((8,)), dma((8,)), dma((6,)), dma((6,)), dma((4,)), dma((4,)),
+            scratch((128, 512), BF16),
+            dma((4,)), dma, dma, dma, dma, dma((4,)), dma((4,)), dma((6,)), dma((6,)), dma((4,)), dma((4,)),
+            dma((6,)), dma((6,)),
         ],
         compiler_params=pltpu.CompilerParams(
             collective_id=1, has_side_effects=True, vmem_limit_bytes=60 * 1024 * 1024

time: 63.9 us -> 47.3 us (0.74)
  Pallas kernels: 58.2 us -> 41.6 us
    pallas_call x1, Pallas kernels: 58.2 us -> 41.6 us  [shards(): pl.pallas_call(kernel, out_shape=(jax.ShapeDtypeStruct(tracers.shape, F32...]
where the time goes in v1:
time: 47.3 us; the launch traced here: 47.1 us
  Pallas kernels  41.6 us (88%)
  local copies, waits for them, and re-layouts  4.19 us (9%)
  between operations  1.3 us (3%)
    pallas_call x1, Pallas kernels, shards(): pl.pallas_call(kernel, out_shape=(jax.ShapeDtypeStruct(tracers.shape, F32...  41.6 us
    unnamed x4, local copies, waits for them, and re-layouts  4.19 us

profile of v1, /device:TPU:1, one launch (start us, length us, event | category | flops | bytes accessed | tf_op | source)
XLA Modules:
  0.0 47.1 jit_solution(12558731431380283479)
XLA Ops:
  1.3 41.6 %shard_map.122 = (f32[2,10,64,512]{3,2,1,0:T(8,128)}, f32[20,2,128]{2,1,0:T(2,128)}) custom-call(f32[2,10,64,512]{3,2,1,0:T(8,128)} %tr_hbm.1, f32[3,10,64,512]{3,2,1,0:T(8,128)} %di_hbm.1, f32[2,10,64,512]{3,2,1,0:T(8,128)} %ve_hbm.1, s32[10,64,512]{2,1,0:T(8,128)} %wet_hbm.1, f32[128,128]{1,0:T(8,128)} %rows_ref.1, s32[1,128]{1,0:T(1,128)} %bitcast.3, ...), custom_call_target="tpu_custom_call" | custom-call | tf_op jit(solution)/shard_map/pallas_call | solution.py:455
  42.9 0.0 copy-start
  42.9 3.6 %copy.16 = f32[2,10,64,512]{3,2,1,0:T(8,128)} copy(f32[2,10,64,512]{3,2,1,0:T(8,128)} %get-tuple-element.4) | data formatting | bytes 5242880
  46.4 0.0 copy-done
  46.5 0.6 %copy.17 = f32[20,2,128]{2,1,0:T(2,128)} copy(f32[20,2,128]{2,1,0:T(2,128)S(1)} %copy-done) | data formatting | bytes 40960
Async XLA Ops:
  42.9 3.6 %copy-start = (f32[20,2,128]{2,1,0:T(2,128)S(1)}, f32[20,2,128]{2,1,0:T(2,128)}, u32[]{:S(2)}) copy-start(f32[20,2,128]{2,1,0:T(2,128)} %get-tuple-element.5) | copy-start | bytes 61444

commit v2 on v1

--- a/solution.py
+++ b/solution.py
@@ -50,11 +50,12 @@
 
 
 def kernel(
-    tr_hbm, di_hbm, ve_hbm, wet_hbm, rows_ref, dest_ref, cols_ref, count_ref, fval_ref, fpos_ref, fdest_ref,
+    tr_hbm, di_hbm, ve_hbm, wet_hbm, rows_hbm, dest_hbm, cols_hbm, count_hbm, fval_hbm, fpos_hbm, fdest_hbm,
     out_ref, fout_ref,
     c0, c1, dx, vx, wi, wf, vbuf, packs, from_w, from_e, from_nw, from_sw, from_ne, from_se,
     msg, mid, got, fsend, fgot, amat, hot, spread,
-    load_sem, p1_s, p1_r, p2_s, p2_r, ns_s, ns_r, ew_s, ew_r, fl_s, fl_r, row_s, row_r,
+    rows_ref, dest_ref, cols_ref, count_ref, fval_ref, fpos_ref, fdest_ref,
+    small_sem, load_sem, p1_s, p1_r, p2_s, p2_r, ns_s, ns_r, ew_s, ew_r, fl_s, fl_r, row_s, row_r,
 ):
     lon, lat, u, v = places()
     east, west = ((lon + 1) % 32, lat), ((lon + 31) % 32, lat)
@@ -62,6 +63,16 @@
     ne, se = (east[0], north[1]), (east[0], south[1])
     nw, sw = (west[0], north[1]), (west[0], south[1])
     barrier = pltpu.get_barrier_semaphore()
+
+    smalls = [
+        pltpu.make_async_copy(src, dst, small_sem.at[i])
+        for i, (src, dst) in enumerate((
+            (rows_hbm, rows_ref), (dest_hbm, dest_ref), (cols_hbm, cols_ref), (count_hbm, count_ref),
+            (fval_hbm, fval_ref), (fpos_hbm, fpos_ref), (fdest_hbm, fdest_ref),
+        ))
+    ]
+    for copy in smalls:
+        copy.start()
 
     @pl.loop(1, 8)
     def _(d):
@@ -82,6 +93,9 @@
     ]
     for copy in loads:
         copy.start()
+
+    for copy in smalls:
+        copy.wait()
 
     lane = iota((128, 128), 1)
     sub = iota((128, 128), 0)
@@ -449,16 +463,15 @@
 
 def shards(tracers, diffusivity, velocity, wet_mask, argo_rows, argo_dest, argo_cols, argo_count, float_values, float_pos, float_dest):
     vmem = pl.BlockSpec(memory_space=pltpu.VMEM)
-    hbm = pl.BlockSpec(memory_space=pl.ANY)
-    smem = pl.BlockSpec(memory_space=pltpu.SMEM)
+    hbm = pl.BlockSpec(memory_space=pltpu.HBM)
     dma, scratch = pltpu.SemaphoreType.DMA, pltpu.VMEM
     return pl.pallas_call(
         kernel,
         out_shape=(
-            jax.ShapeDtypeStruct(tracers.shape, F32),
-            jax.ShapeDtypeStruct((20, 2, 128), F32),
+            pltpu.VMEM(tracers.shape, F32),
+            pltpu.VMEM((20, 2, 128), F32),
         ),
-        in_specs=[hbm] * 4 + [vmem, vmem, vmem, smem, vmem, vmem, vmem],
+        in_specs=[hbm] * 11,
         out_specs=(vmem, vmem),
         scratch_shapes=[
             scratch((2, LEVELS + 1, EH, EW), F32),
@@ -483,11 +496,18 @@
             scratch((H * 21, 512), BF16),
             scratch((W, 2560), BF16),
             scratch((128, 512), BF16),
-            dma((4,)), dma, dma, dma, dma, dma((4,)), dma((4,)), dma((6,)), dma((6,)), dma((4,)), dma((4,)),
+            scratch((128, 128), F32),
+            scratch((1, 128), I32),
+            scratch((1, 128), I32),
+            pltpu.SMEM((1,), I32),
+            scratch((16, 2, 128), F32),
+            scratch((16, 2, 128), F32),
+            scratch((1, 16), I32),
+            dma((7,)), dma((4,)), dma, dma, dma, dma, dma((4,)), dma((4,)), dma((6,)), dma((6,)), dma((4,)), dma((4,)),
             dma((6,)), dma((6,)),
         ],
         compiler_params=pltpu.CompilerParams(
-            collective_id=1, has_side_effects=True, vmem_limit_bytes=60 * 1024 * 1024
+            collective_id=1, has_side_effects=True, vmem_limit_bytes=61 * 1024 * 1024
         ),
     )(
         tracers, diffusivity, velocity, wet_mask, argo_rows, argo_dest.reshape(1, -1), argo_cols.reshape(1, -1),

time: 47.3 us -> 43.4 us (0.918)
  local copies, waits for them, and re-layouts: 4.19 us -> 2.1 us
  Pallas kernels: 41.6 us -> 39.9 us
    unnamed x4 -> x2, local copies, waits for them, and re-layouts: 4.19 us -> 2.1 us
    pallas_call x1, Pallas kernels: 41.6 us -> 39.9 us  [shards(): pl.pallas_call(kernel, out_shape=(pltpu.VMEM(tracers.shape, F32), pltpu.V...]
where the time goes in v2:
time: 43.4 us; the launch traced here: 43.3 us
  Pallas kernels  39.9 us (92%)
  local copies, waits for them, and re-layouts  2.1 us (5%)
  between operations  1.29 us (3%)
    pallas_call x1, Pallas kernels, shards(): pl.pallas_call(kernel, out_shape=(pltpu.VMEM(tracers.shape, F32), pltpu.V...  39.9 us
    unnamed x2, local copies, waits for them, and re-layouts  2.1 us

profile of v2, /device:TPU:1, one launch (start us, length us, event | category | flops | bytes accessed | tf_op | source)
XLA Modules:
  0.0 43.3 jit_solution(16235029460610838148)
XLA Ops:
  1.3 39.9 %shard_map.122 = (f32[2,10,64,512]{3,2,1,0:T(8,128)S(1)}, f32[20,2,128]{2,1,0:T(2,128)S(1)}) custom-call(f32[2,10,64,512]{3,2,1,0:T(8,128)} %tr_hbm.1, f32[3,10,64,512]{3,2,1,0:T(8,128)} %di_hbm.1, f32[2,10,64,512]{3,2,1,0:T(8,128)} %ve_hbm.1, s32[10,64,512]{2,1,0:T(8,128)} %wet_hbm.1, f32[128,128]{1,0:T(8,128)} %rows_hbm.1, s32[1,128]{1,0:T(1,128)} %bitcast.3, ...), custom_call_target="tpu_custom_call" | custom-call | tf_op jit(solution)/shard_map/pallas_call | solution.py:468
  41.2 1.5 %copy.15 = f32[2,10,64,512]{3,2,1,0:T(8,128)} copy(f32[2,10,64,512]{3,2,1,0:T(8,128)S(1)} %get-tuple-element.2) | data formatting | bytes 5242880
  42.7 0.6 %copy.16 = f32[20,2,128]{2,1,0:T(2,128)} copy(f32[20,2,128]{2,1,0:T(2,128)S(1)} %get-tuple-element.3) | data formatting | bytes 40960

commit v3 on v2

--- a/solution.py
+++ b/solution.py
@@ -85,12 +85,17 @@
     for peer in (east, west, north, south, ne, se, nw, sw):
         pl.semaphore_signal(barrier, inc=1, device_id=peer, device_id_type=MESH)
 
-    loads = [
-        pltpu.make_async_copy(di_hbm, dx.at[:, :, pl.ds(0, H), pl.ds(0, W)], load_sem.at[0]),
-        pltpu.make_async_copy(ve_hbm, vx.at[:, :, pl.ds(0, H), pl.ds(0, W)], load_sem.at[1]),
-        pltpu.make_async_copy(wet_hbm, wi.at[:, pl.ds(0, H)], load_sem.at[2]),
-        pltpu.make_async_copy(tr_hbm, c0.at[:, pl.ds(0, LEVELS), pl.ds(0, H), pl.ds(0, W)], load_sem.at[3]),
-    ]
+    rows = pl.ds(0, H)
+    loads = []
+    for a, n in ((0, 128), (384, 128), (128, 256)):
+        lanes = pl.ds(a, n)
+        for src, dst in (
+            (wet_hbm.at[:, :, lanes], wi.at[:, rows, lanes]),
+            (di_hbm.at[:, :, :, lanes], dx.at[:, :, rows, lanes]),
+            (ve_hbm.at[:, :, :, lanes], vx.at[:, :, rows, lanes]),
+            (tr_hbm.at[:, :, :, lanes], c0.at[:, pl.ds(0, LEVELS), rows, lanes]),
+        ):
+            loads.append(pltpu.make_async_copy(src, dst, load_sem.at[len(loads)]))
     for copy in loads:
         copy.start()
 
@@ -168,7 +173,7 @@
         copy.start()
     mid[0] = msg[u]
 
-    for copy in loads:
+    for copy in loads[:8]:
         copy.wait()
 
     lane64 = iota((H, 128), 1)
@@ -179,7 +184,8 @@
             yield q, ((c0, (n, k)), (dx, (0, k)) if n == 0 else (vx, (0, k)), (dx, (1, k)) if n == 0 else (vx, (1, k)), (dx, (2, k)) if n == 0 else (wf, (k,)))[t]
 
     for k in range(LEVELS):
-        wf[k, pl.ds(0, H), wide] = wi[k, pl.ds(0, H)].astype(F32)
+        for a in (0, 384):
+            wf[k, rows, pl.ds(a, 128)] = wi[k, rows, pl.ds(a, 128)].astype(F32)
     for t in range(4):
         acc = jnp.zeros((H, 128), F32)
         for q, (ref, at) in planes_of(t):
@@ -209,6 +215,11 @@
         remote(mid.at[:, t // 4, t % 4], got.at[d], p2_s, p2_r, device_of(u, t)).start()
 
     got[0] = mid[:, v // 4, v % 4]
+
+    for copy in loads[8:]:
+        copy.wait()
+    for k in range(LEVELS):
+        wf[k, rows, pl.ds(128, 256)] = wi[k, rows, pl.ds(128, 256)].astype(F32)
 
     sub8 = iota((8, EW), 0)
 
@@ -503,7 +514,7 @@
             scratch((16, 2, 128), F32),
             scratch((16, 2, 128), F32),
             scratch((1, 16), I32),
-            dma((7,)), dma((4,)), dma, dma, dma, dma, dma((4,)), dma((4,)), dma((6,)), dma((6,)), dma((4,)), dma((4,)),
+            dma((7,)), dma((12,)), dma, dma, dma, dma, dma((4,)), dma((4,)), dma((6,)), dma((6,)), dma((4,)), dma((4,)),
             dma((6,)), dma((6,)),
         ],
         compiler_params=pltpu.CompilerParams(

time: 43.4 us -> 42.8 us (0.986)
  Pallas kernels: 39.9 us -> 39.2 us
    pallas_call x1, Pallas kernels: 39.9 us -> 39.2 us  [shards(): pl.pallas_call(kernel, out_shape=(pltpu.VMEM(tracers.shape, F32), pltpu.V...]
where the time goes in v3:
time: 42.8 us; the launch traced here: 42.6 us
  Pallas kernels  39.2 us (92%)
  local copies, waits for them, and re-layouts  2.1 us (5%)
  between operations  1.29 us (3%)
    pallas_call x1, Pallas kernels, shards(): pl.pallas_call(kernel, out_shape=(pltpu.VMEM(tracers.shape, F32), pltpu.V...  39.2 us
    unnamed x2, local copies, waits for them, and re-layouts  2.1 us

profile of v3, /device:TPU:1, one launch (start us, length us, event | category | flops | bytes accessed | tf_op | source)
XLA Modules:
  0.0 42.6 jit_solution(3312227273993185003)
XLA Ops:
  1.3 39.2 %shard_map.122 = (f32[2,10,64,512]{3,2,1,0:T(8,128)S(1)}, f32[20,2,128]{2,1,0:T(2,128)S(1)}) custom-call(f32[2,10,64,512]{3,2,1,0:T(8,128)} %tr_hbm.1, f32[3,10,64,512]{3,2,1,0:T(8,128)} %di_hbm.1, f32[2,10,64,512]{3,2,1,0:T(8,128)} %ve_hbm.1, s32[10,64,512]{2,1,0:T(8,128)} %wet_hbm.1, f32[128,128]{1,0:T(8,128)} %rows_hbm.1, s32[1,128]{1,0:T(1,128)} %bitcast.3, ...), custom_call_target="tpu_custom_call" | custom-call | tf_op jit(solution)/shard_map/pallas_call | solution.py:479
  40.5 1.5 %copy.15 = f32[2,10,64,512]{3,2,1,0:T(8,128)} copy(f32[2,10,64,512]{3,2,1,0:T(8,128)S(1)} %get-tuple-element.2) | data formatting | bytes 5242880
  42.0 0.6 %copy.16 = f32[20,2,128]{2,1,0:T(2,128)} copy(f32[20,2,128]{2,1,0:T(2,128)S(1)} %get-tuple-element.3) | data formatting | bytes 40960

commit v4 on v3

--- a/solution.py
+++ b/solution.py
@@ -420,9 +420,9 @@
                 flux_u = load(vbuf, (n,), i)
                 rows = pl.ds(8 * i, 8)
                 for j in range(tiles):
-                    vbuf[n, rows, pl.ds(128 * j, 128)] = flux_v[j]
                     if last and j == tiles - 1:
                         continue
+                    vbuf[n, rows, pl.ds(128 * j, 128)] = flux_v[j]
                     new = here[j] + (flux_n[j] - jnp.where(first_row, below[i, n][j], dropped[j]))
                     new = new + (flux[j] - jnp.where(first_lane, moved[j - 1], moved[j])) + (flux_v[j] - flux_u[j])
                     dst[n, k, rows, pl.ds(128 * j, 128)] = new
@@ -443,7 +443,7 @@
                         work(*chunks[at - stage * GAP])
 
     for number, (src, dst) in enumerate(((c0, c1), (c1, c0), (c0, out_ref))):
-        vbuf[...] = jnp.zeros((2, EH, EW), F32)
+        vbuf[:, pl.ds(0, H)] = jnp.zeros((2, H, EW), F32)
         sweep(src, dst, number == 2, [(1, 6)])
         for copy in rims[number]:
             copy.wait()

time: 42.8 us -> 42.8 us (level)
  no operation moved by 1% of the time
where the time goes in v4:
time: 42.8 us; the launch traced here: 42.6 us
  Pallas kernels  39.3 us (92%)
  local copies, waits for them, and re-layouts  2.1 us (5%)
  between operations  1.29 us (3%)
    pallas_call x1, Pallas kernels, shards(): pl.pallas_call(kernel, out_shape=(pltpu.VMEM(tracers.shape, F32), pltpu.V...  39.3 us
    unnamed x2, local copies, waits for them, and re-layouts  2.1 us

profile of v4, /device:TPU:1, one launch (start us, length us, event | category | flops | bytes accessed | tf_op | source)
XLA Modules:
  0.0 42.6 jit_solution(12799951225327912714)
XLA Ops:
  1.3 39.3 %shard_map.122 = (f32[2,10,64,512]{3,2,1,0:T(8,128)S(1)}, f32[20,2,128]{2,1,0:T(2,128)S(1)}) custom-call(f32[2,10,64,512]{3,2,1,0:T(8,128)} %tr_hbm.1, f32[3,10,64,512]{3,2,1,0:T(8,128)} %di_hbm.1, f32[2,10,64,512]{3,2,1,0:T(8,128)} %ve_hbm.1, s32[10,64,512]{2,1,0:T(8,128)} %wet_hbm.1, f32[128,128]{1,0:T(8,128)} %rows_hbm.1, s32[1,128]{1,0:T(1,128)} %bitcast.3, ...), custom_call_target="tpu_custom_call" | custom-call | tf_op jit(solution)/shard_map/pallas_call | solution.py:479
  40.5 1.5 %copy.15 = f32[2,10,64,512]{3,2,1,0:T(8,128)} copy(f32[2,10,64,512]{3,2,1,0:T(8,128)S(1)} %get-tuple-element.2) | data formatting | bytes 5242880
  42.0 0.6 %copy.16 = f32[20,2,128]{2,1,0:T(2,128)} copy(f32[20,2,128]{2,1,0:T(2,128)S(1)} %get-tuple-element.3) | data formatting | bytes 40960
